TPU v7x, 32 devices: a whole 2x2x4 slice. The times are simulated.
32 devices in a mesh: energy: 8 (over y, x, core), momentum: 4 (over z).
Axes of the slice: x: 2, y: 2, z: 4, core: 2. Of those that a mesh axis runs over, the one named last changes fastest.
Arguments:
- green_blocks: float32 [2, 8, 4, 200, 256], P(None, 'energy', 'momentum'), may hold values from -6 to 6
- couple_matrix: float32 [3, 100, 256], P(None, None, ('energy', 'momentum')), may hold values from -1.8 to 1.8
- occupation: float32 [3], replicated, may hold values from 0.1 to 3
- energy_shift: int32 [3], replicated, may hold values from 1 to 7, as said below
- branch_weight: float32 [4, 3], replicated, may hold values from 0.3 to 3
- pair_branch: int32 [4, 4], replicated, may hold values from 0 to 3
Outputs:
- self_energy: float32 [2, 8, 4, 200, 256], P(None, 'energy', 'momentum')
Inputs may be any that keep to these rules, and one draw needn't show every extreme that they name: `energy_shift`: the branches' shifts are distinct.
All inputs are finite; a program needn't handle non-finite values.
Results may differ from a plain program's by a relative error of at most 0.0001.
Values sent between devices are 32-bit elements; how exact they have to be, the bound alone decides.
A program may use at most 192 MiB of HBM per device.

v0:
```python
import functools

import jax
import jax.numpy as jnp
from jax import lax
from jax.experimental import pallas as pl
from jax.experimental.pallas import tpu as pltpu
from jax.sharding import PartitionSpec as P

ORB = 10
PAIRS = ORB * ORB
LANES = 128
ROWS = 8
GROUP = 8
PIECES = LANES // GROUP
QUARTERS = 4
STEPS = PAIRS // QUARTERS
SLOT = 32
CHUNKS = SLOT // ROWS
MESH = pl.DeviceIdType.MESH


def swap_groups(arrays, lane, width):
    arrays = list(arrays)
    bit = 1
    while bit < len(arrays):
        low = ((lane // width) & bit) == 0
        for p in range(len(arrays)):
            if p & bit:
                continue
            a, b = arrays[p], arrays[p | bit]
            arrays[p] = jnp.where(low, a, pltpu.roll(b, bit * width, 1))
            arrays[p | bit] = jnp.where(low, pltpu.roll(a, LANES - bit * width, 1), b)
        bit *= 2
    return arrays


def total_of(terms):
    while len(terms) > 1:
        paired = [terms[i] + terms[i + 1] for i in range(0, len(terms) - 1, 2)]
        terms = paired + ([terms[-1]] if len(terms) % 2 else [])
    return terms[0]


def piece_rows(piece):
    quarter, kind, part = piece // 4, (piece // 2) % 2, piece % 2
    return kind * 2 * PAIRS + part * PAIRS + quarter


def kernel(
    n_energy,
    n_moment,
    modes,
    shift_ref,
    occupation_ref,
    weight_ref,
    branch_ref,
    couple_ref,
    green_ref,
    out_ref,
    inside,
    packed,
    arrived,
    mixed,
    coupling,
    coef,
    right_done,
    both_done,
    back,
    returned,
    outside,
    local_sem,
    send_sem,
    recv_sem,
    send_back_sem,
    recv_back_sem,
):
    count = n_energy * n_moment
    tiles = green_ref.shape[2] // LANES
    groups = n_moment // QUARTERS
    heights = n_energy // ROWS
    my_energy = lax.axis_index("energy")
    my_moment = lax.axis_index("momentum")

    def slot_of(energy, moment):
        return pl.multiple_of((moment * n_energy + energy) * SLOT, SLOT)

    def slot_of_rank(rank):
        return slot_of(rank // n_moment, rank % n_moment)

    def partner(offset, sign):
        energy = lax.rem(my_energy + sign * (offset // n_moment) + n_energy, n_energy)
        moment = lax.rem(my_moment + sign * (offset % n_moment) + n_moment, n_moment)
        return energy, moment

    loads = []
    for kind in range(2):
        for tile in range(tiles):
            load = pltpu.make_async_copy(
                green_ref.at[kind, :, pl.ds(tile * LANES, LANES)],
                inside.at[tile, pl.ds(kind * 2 * PAIRS, 2 * PAIRS)],
                local_sem.at[kind, tile],
            )
            load.start()
            loads.append(load)

    barrier = pltpu.get_barrier_semaphore()

    def greet(offset, carry):
        energy, moment = partner(offset, 1)
        pl.semaphore_signal(
            barrier, inc=1, device_id={"energy": energy, "momentum": moment}, device_id_type=MESH
        )
        return carry

    lax.fori_loop(1, count, greet, 0)

    lane = lax.broadcasted_iota(jnp.int32, (ROWS, LANES), 1)

    for load in loads:
        load.wait()

    def pack(tile, carry):
        for chunk in range(CHUNKS):
            pieces = [
                inside[
                    tile,
                    pl.ds(piece_rows(p) + QUARTERS * ROWS * chunk, ROWS, stride=QUARTERS),
                    :,
                ]
                for p in range(PIECES)
            ]
            for g, value in enumerate(swap_groups(pieces, lane, GROUP)):
                row = slot_of_rank(tile * PIECES + g) + chunk * ROWS
                packed[pl.ds(pl.multiple_of(row, ROWS), ROWS), :] = value
        return carry

    lax.fori_loop(0, tiles, pack, 0)

    pl.semaphore_wait(barrier, count - 1)

    mine = slot_of(my_energy, my_moment)

    def outgoing(source, target, sends, receives, offset):
        energy, moment = partner(offset, 1)
        return pltpu.make_async_remote_copy(
            src_ref=source.at[pl.ds(slot_of(energy, moment), STEPS)],
            dst_ref=target.at[pl.ds(mine, STEPS)],
            send_sem=sends.at[offset],
            recv_sem=receives.at[offset],
            device_id={"energy": energy, "momentum": moment},
            device_id_type=MESH,
        )

    def incoming(source, target, sends, receives, offset):
        energy, moment = partner(offset, -1)
        return pltpu.make_async_remote_copy(
            src_ref=source.at[pl.ds(mine, STEPS)],
            dst_ref=target.at[pl.ds(slot_of(energy, moment), STEPS)],
            send_sem=sends.at[offset],
            recv_sem=receives.at[offset],
            device_id={"energy": energy, "momentum": moment},
            device_id_type=MESH,
        )

    def exchange_start(source, target, sends, receives):
        def step(offset, carry):
            outgoing(source, target, sends, receives, offset).start()
            return carry

        lax.fori_loop(1, count, step, 0)
        own = pltpu.make_async_copy(
            source.at[pl.ds(mine, STEPS)], target.at[pl.ds(mine, STEPS)], receives.at[0]
        )
        own.start()
        return own

    def exchange_wait(source, target, sends, receives, own):
        def step(offset, carry):
            incoming(source, target, sends, receives, offset).wait_recv()
            return carry

        own.wait()
        lax.fori_loop(1, count, step, 0)

    def sends_wait(source, target, sends, receives):
        def step(offset, carry):
            outgoing(source, target, sends, receives, offset).wait_send()
            return carry

        lax.fori_loop(1, count, step, 0)

    there = (packed, arrived, send_sem, recv_sem)
    own = exchange_start(*there)

    spread = (
        lax.broadcasted_iota(jnp.int32, (GROUP, LANES), 1) % GROUP
        == lax.broadcasted_iota(jnp.int32, (GROUP, LANES), 0)
    ).astype(jnp.float32)
    for mode in range(modes):
        wide = jnp.dot(
            couple_ref[mode],
            spread,
            precision=lax.Precision.HIGHEST,
            preferred_element_type=jnp.float32,
        )
        coupling[pl.ds(mode * PAIRS, PAIRS)] = jnp.broadcast_to(
            wide[:, None, :], (PAIRS, ROWS, LANES)
        )

    lane_moment = lane // (LANES // QUARTERS)
    for mode in range(modes):
        for kg in range(groups):
            for jg in range(groups):
                for turn in range(QUARTERS):
                    value = jnp.zeros((ROWS, LANES), jnp.float32)
                    for kl in range(QUARTERS):
                        k = kg * QUARTERS + kl
                        j = jg * QUARTERS + (kl - turn) % QUARTERS
                        weight = weight_ref[branch_ref[k, j], mode] / n_moment
                        value = jnp.where(lane_moment == kl, weight, value)
                    coef[mode, kg, jg, turn] = value
    kind = ((lane // (2 * GROUP)) % 2).astype(jnp.float32)

    empty = jnp.zeros((n_energy, LANES), jnp.float32)
    for mode in range(modes):
        for kg in range(groups):

            def clear(pair, carry):
                row = pl.multiple_of(pair * 2 * n_energy, ROWS)
                mixed[mode, kg, pl.ds(row, n_energy), :] = empty
                return carry

            lax.fori_loop(0, PAIRS + 1, clear, 0)

    exchange_wait(*there, own)

    def mix_step(step, carry):
        for height in range(heights):
            quarters = []
            for jg in range(groups):
                values = [
                    arrived[
                        pl.ds(
                            ((jg * QUARTERS + jl) * n_energy + height * ROWS) * SLOT + step,
                            ROWS,
                            stride=SLOT,
                        ),
                        :,
                    ]
                    for jl in range(QUARTERS)
                ]
                quarters.append(swap_groups(values, lane, LANES // QUARTERS))
            for q in range(QUARTERS):
                turned = [
                    [quarters[jg][q]]
                    + [pltpu.roll(quarters[jg][q], turn * GROUP * 4, 1) for turn in range(1, QUARTERS)]
                    for jg in range(groups)
                ]
                row = (QUARTERS * step + q) * 2 * n_energy + n_energy + height * ROWS
                row = pl.multiple_of(row, ROWS)
                for mode in range(modes):
                    for kg in range(groups):
                        mixed[mode, kg, pl.ds(row, ROWS), :] = total_of(
                            [
                                turned[jg][turn] * coef[mode, kg, jg, turn]
                                for jg in range(groups)
                                for turn in range(QUARTERS)
                            ]
                        )
        return carry

    lax.fori_loop(0, STEPS, mix_step, 0)

    for mode in range(modes):
        shift = shift_ref[mode]
        upper_coef = occupation_ref[mode] + 1.0 - kind
        lower_coef = occupation_ref[mode] + kind
        for kg in range(groups):
            for height in range(heights):

                def right_step(row, carry):
                    values = []
                    for col in range(ORB):
                        first = (row * ORB + col) * 2 * n_energy + n_energy + height * ROWS
                        upper = mixed[mode, kg, pl.ds(first + shift, ROWS), :]
                        lower = mixed[mode, kg, pl.ds(first - shift, ROWS), :]
                        values.append(upper_coef * upper + lower_coef * lower)
                    for n in range(ORB):
                        right_done[mode, kg, height, row * ORB + n] = total_of(
                            [
                                values[col] * coupling[mode * PAIRS + n * ORB + col]
                                for col in range(ORB)
                            ]
                        )
                    return carry

                lax.fori_loop(0, ORB, right_step, 0)

    for kg in range(groups):
        for height in range(heights):

            def left_step(n, carry):
                values = [
                    [right_done[mode, kg, height, row * ORB + n] for row in range(ORB)]
                    for mode in range(modes)
                ]
                for i in range(ORB):
                    both_done[kg, height, i * ORB + n] = total_of(
                        [
                            values[mode][row] * coupling[mode * PAIRS + i * ORB + row]
                            for mode in range(modes)
                            for row in range(ORB)
                        ]
                    )
                return carry

            lax.fori_loop(0, ORB, left_step, 0)

    def unmix_step(step, carry):
        for kg in range(groups):
            for height in range(heights):
                values = [both_done[kg, height, QUARTERS * step + q] for q in range(QUARTERS)]
                for kl, value in enumerate(swap_groups(values, lane, LANES // QUARTERS)):
                    row = ((kg * QUARTERS + kl) * n_energy + height * ROWS) * SLOT + step
                    back[pl.ds(row, ROWS, stride=SLOT), :] = value
        return carry

    lax.fori_loop(0, STEPS, unmix_step, 0)

    home = (back, returned, send_back_sem, recv_back_sem)
    own = exchange_start(*home)
    sends_wait(*there)
    exchange_wait(*home, own)

    def unpack(tile, carry):
        for chunk in range(CHUNKS):
            values = []
            for g in range(PIECES):
                row = slot_of_rank(tile * PIECES + g) + chunk * ROWS
                values.append(returned[pl.ds(pl.multiple_of(row, ROWS), ROWS), :])
            kept = min(ROWS, STEPS - chunk * ROWS)
            for p, value in enumerate(swap_groups(values, lane, GROUP)):
                first = piece_rows(p) + QUARTERS * ROWS * chunk
                if kept == ROWS:
                    outside[tile, pl.ds(first, ROWS, stride=QUARTERS), :] = value
                else:
                    outside[tile, pl.ds(first, kept), :] = value[:kept]
        return carry

    lax.fori_loop(0, tiles, unpack, 0)

    stores = []
    for kind_index in range(2):
        for tile in range(tiles):
            store = pltpu.make_async_copy(
                outside.at[tile, pl.ds(kind_index * 2 * PAIRS, 2 * PAIRS)],
                out_ref.at[kind_index, :, pl.ds(tile * LANES, LANES)],
                local_sem.at[kind_index, tile],
            )
            store.start()
            stores.append(store)
    sends_wait(*home)
    for store in stores:
        store.wait()


def on_device(green_blocks, couple_matrix, occupation, energy_shift, branch_weight, pair_branch):
    n_energy = lax.axis_size("energy")
    n_moment = lax.axis_size("momentum")
    modes = couple_matrix.shape[0]
    width, atoms = green_blocks.shape[3:]
    count = n_energy * n_moment
    tiles = atoms // LANES
    groups = n_moment // QUARTERS
    heights = n_energy // ROWS
    assert green_blocks.shape[1:3] == (1, 1) and width == 2 * PAIRS
    assert couple_matrix.shape[2] == GROUP and STEPS % ROWS == 1
    slots = pltpu.VMEM((count * SLOT, LANES), jnp.float32)
    smem = pl.BlockSpec(memory_space=pltpu.SMEM)
    spare = QUARTERS * (SLOT - STEPS) + QUARTERS
    result = pl.pallas_call(
        functools.partial(kernel, n_energy, n_moment, modes),
        out_shape=jax.ShapeDtypeStruct((2, width, atoms), jnp.float32),
        in_specs=[
            smem,
            smem,
            smem,
            smem,
            pl.BlockSpec(memory_space=pltpu.VMEM),
            pl.BlockSpec(memory_space=pl.ANY),
        ],
        out_specs=pl.BlockSpec(memory_space=pl.ANY),
        scratch_shapes=[
            pltpu.VMEM((tiles, 2 * width + spare, LANES), jnp.float32),
            slots,
            slots,
            pltpu.VMEM((modes, groups, (2 * PAIRS + 1) * n_energy, LANES), jnp.float32),
            pltpu.VMEM((modes * PAIRS, ROWS, LANES), jnp.float32),
            pltpu.VMEM((modes, groups, groups, QUARTERS, ROWS, LANES), jnp.float32),
            pltpu.VMEM((modes, groups, heights, PAIRS, ROWS, LANES), jnp.float32),
            pltpu.VMEM((groups, heights, PAIRS, ROWS, LANES), jnp.float32),
            slots,
            slots,
            pltpu.VMEM((tiles, 2 * width, LANES), jnp.float32),
            pltpu.SemaphoreType.DMA((2, tiles)),
            pltpu.SemaphoreType.DMA((count,)),
            pltpu.SemaphoreType.DMA((count,)),
            pltpu.SemaphoreType.DMA((count,)),
            pltpu.SemaphoreType.DMA((count,)),
        ],
        compiler_params=pltpu.CompilerParams(
            collective_id=0, has_side_effects=True, vmem_limit_bytes=48 * 1024 * 1024
        ),
        name="self_energy",
    )(
        energy_shift,
        occupation,
        branch_weight,
        pair_branch,
        couple_matrix,
        green_blocks.reshape(2, width, atoms),
    )
    return result.reshape(green_blocks.shape)


def solution(mesh):
    in_specs = (
        P(None, "energy", "momentum", None, None),
        P(None, None, ("energy", "momentum")),
        P(),
        P(),
        P(),
        P(),
    )
    out_specs = P(None, "energy", "momentum", None, None)
    return jax.shard_map(
        on_device, mesh=mesh, in_specs=in_specs, out_specs=out_specs, check_vma=False
    )
```

profile of v0, /device:TPU:0, one launch (start us, length us, event | category | flops | bytes accessed | tf_op | source)
XLA Modules:
  0.0 46.9 jit_solution(7248723336650918538)
XLA Ops:
  0.0 0.0 copy-start.1
  0.0 0.0 copy-start.2
  0.0 0.0 copy-start.3
  0.0 0.0 copy-start.4
  0.0 0.9 %copy.7.couple_ref = f32[3,100,8]{2,1,0:T(8,128)S(1)} copy(f32[3,100,8]{1,2,0:T(8,128)} %param.7) | data formatting | bytes 19200 | tf_op args[1]
  0.9 0.0 copy-done.1
  0.9 0.0 copy-done.2
  0.9 0.0 copy-done.3
  0.9 0.0 copy-done.4
  0.9 0.0 copy-start
  0.9 1.0 %copy-done = f32[2,1,1,200,256]{4,3,2,1,0:T(8,128)S(1)} copy-done((f32[2,1,1,200,256]{4,3,2,1,0:T(8,128)S(1)}, f32[2,1,1,200,256]{4,3,2,1,0:T(8,128)}, u32[]{:S(2)}) %copy-start) | copy-done | bytes 409624
  1.9 44.2 %self_energy.1 = f32[2,200,256]{2,1,0:T(8,128)S(1)} custom-call(s32[3]{0:T(128)S(1)} %copy-done.3, f32[3]{0:T(128)S(1)} %copy-done.4, f32[4,3]{1,0:T(4,128)S(1)} %copy-done.1, s32[4,4]{1,0:T(4,128)S(1)} %copy-done.2, f32[3,100,8]{2,1,0:T(8,128)S(1)} %copy.7.couple_ref, f32[2,200,256]{2,1,0:T(8,128)S(1)} %bitcast.5), custom_call_target="tpu_custom_call" | custom-call | tf_op jit(solution)/shard_map/self_energy/pallas_call | solution.py:382
  46.2 0.8 %copy.10 = f32[2,1,1,200,256]{4,3,2,1,0:T(8,128)} copy(f32[2,1,1,200,256]{4,3,2,1,0:T(8,128)S(1)} %bitcast.4) | data formatting | bytes 819200
Async XLA Ops:
  0.0 0.9 %copy-start.1 = (f32[4,3]{1,0:T(4,128)S(1)}, f32[4,3]{1,0:T(4,128)}, u32[]{:S(2)}) copy-start(f32[4,3]{1,0:T(4,128)} %weight_ref.1) | copy-start | bytes 148
  0.0 0.9 %copy-start.2 = (s32[4,4]{1,0:T(4,128)S(1)}, s32[4,4]{1,0:T(4,128)}, u32[]{:S(2)}) copy-start(s32[4,4]{1,0:T(4,128)} %branch_ref.1) | copy-start | bytes 196
  0.0 0.9 %copy-start.3 = (s32[3]{0:T(128)S(1)}, s32[3]{0:T(128)}, u32[]{:S(2)}) copy-start(s32[3]{0:T(128)} %shift_ref.1) | copy-start | bytes 40
  0.0 0.9 %copy-start.4 = (f32[3]{0:T(128)S(1)}, f32[3]{0:T(128)}, u32[]{:S(2)}) copy-start(f32[3]{0:T(128)} %occupation_ref.1) | copy-start | bytes 40
  0.9 1.0 %copy-start = (f32[2,1,1,200,256]{4,3,2,1,0:T(8,128)S(1)}, f32[2,1,1,200,256]{4,3,2,1,0:T(8,128)}, u32[]{:S(2)}) copy-start(f32[2,1,1,200,256]{4,3,2,1,0:T(8,128)} %param.6) | copy-start | bytes 1228804
where the time goes:
time: 47.1 us; the launch traced here: 46.9 us
  Pallas kernels  44.2 us (94%)
  local copies, waits for them, and re-layouts  2.65 us (6%)
    pallas_call x1, Pallas kernels, on_device(): pl.pallas_call(functools.partial(kernel, n_energy, n_moment, modes), out_...  44.2 us
    unnamed x12, local copies, waits for them, and re-layouts  2.65 us

commit v1 on v0

--- a/solution.py
+++ b/solution.py
@@ -17,6 +17,7 @@
 STEPS = PAIRS // QUARTERS
 SLOT = 32
 CHUNKS = SLOT // ROWS
+UNROLL = 5
 MESH = pl.DeviceIdType.MESH
 
 
@@ -51,13 +52,18 @@
     n_energy,
     n_moment,
     modes,
+    shift_hbm,
+    occupation_hbm,
+    weight_hbm,
+    branch_hbm,
+    couple_hbm,
+    green_ref,
+    out_ref,
     shift_ref,
     occupation_ref,
     weight_ref,
     branch_ref,
     couple_ref,
-    green_ref,
-    out_ref,
     inside,
     packed,
     arrived,
@@ -70,6 +76,7 @@
     returned,
     outside,
     local_sem,
+    small_sem,
     send_sem,
     recv_sem,
     send_back_sem,
@@ -103,6 +110,20 @@
             )
             load.start()
             loads.append(load)
+
+    small_loads = []
+    for index, (source, target) in enumerate(
+        (
+            (couple_hbm, couple_ref),
+            (shift_hbm, shift_ref),
+            (occupation_hbm, occupation_ref),
+            (weight_hbm, weight_ref),
+            (branch_hbm, branch_ref),
+        )
+    ):
+        load = pltpu.make_async_copy(source, target, small_sem.at[index])
+        load.start()
+        small_loads.append(load)
 
     barrier = pltpu.get_barrier_semaphore()
 
@@ -193,14 +214,17 @@
     there = (packed, arrived, send_sem, recv_sem)
     own = exchange_start(*there)
 
+    for load in small_loads:
+        load.wait()
     spread = (
         lax.broadcasted_iota(jnp.int32, (GROUP, LANES), 1) % GROUP
         == lax.broadcasted_iota(jnp.int32, (GROUP, LANES), 0)
     ).astype(jnp.float32)
     for mode in range(modes):
-        wide = jnp.dot(
+        wide = lax.dot_general(
             couple_ref[mode],
             spread,
+            (((0,), (0,)), ((), ())),
             precision=lax.Precision.HIGHEST,
             preferred_element_type=jnp.float32,
         )
@@ -231,7 +255,7 @@
                 mixed[mode, kg, pl.ds(row, n_energy), :] = empty
                 return carry
 
-            lax.fori_loop(0, PAIRS + 1, clear, 0)
+            lax.fori_loop(0, PAIRS + 1, clear, 0, unroll=True)
 
     exchange_wait(*there, own)
 
@@ -270,7 +294,7 @@
                         )
         return carry
 
-    lax.fori_loop(0, STEPS, mix_step, 0)
+    lax.fori_loop(0, STEPS, mix_step, 0, unroll=UNROLL)
 
     for mode in range(modes):
         shift = shift_ref[mode]
@@ -295,7 +319,7 @@
                         )
                     return carry
 
-                lax.fori_loop(0, ORB, right_step, 0)
+                lax.fori_loop(0, ORB, right_step, 0, unroll=2)
 
     for kg in range(groups):
         for height in range(heights):
@@ -326,7 +350,7 @@
                     back[pl.ds(row, ROWS, stride=SLOT), :] = value
         return carry
 
-    lax.fori_loop(0, STEPS, unmix_step, 0)
+    lax.fori_loop(0, STEPS, unmix_step, 0, unroll=UNROLL)
 
     home = (back, returned, send_back_sem, recv_back_sem)
     own = exchange_start(*home)
@@ -377,21 +401,18 @@
     assert green_blocks.shape[1:3] == (1, 1) and width == 2 * PAIRS
     assert couple_matrix.shape[2] == GROUP and STEPS % ROWS == 1
     slots = pltpu.VMEM((count * SLOT, LANES), jnp.float32)
-    smem = pl.BlockSpec(memory_space=pltpu.SMEM)
     spare = QUARTERS * (SLOT - STEPS) + QUARTERS
     result = pl.pallas_call(
         functools.partial(kernel, n_energy, n_moment, modes),
         out_shape=jax.ShapeDtypeStruct((2, width, atoms), jnp.float32),
-        in_specs=[
-            smem,
-            smem,
-            smem,
-            smem,
-            pl.BlockSpec(memory_space=pltpu.VMEM),
-            pl.BlockSpec(memory_space=pl.ANY),
-        ],
+        in_specs=[pl.BlockSpec(memory_space=pl.ANY)] * 6,
         out_specs=pl.BlockSpec(memory_space=pl.ANY),
         scratch_shapes=[
+            pltpu.SMEM(energy_shift.shape, jnp.int32),
+            pltpu.SMEM(occupation.shape, jnp.float32),
+            pltpu.SMEM(branch_weight.shape, jnp.float32),
+            pltpu.SMEM(pair_branch.shape, jnp.int32),
+            pltpu.VMEM((modes, GROUP, PAIRS), jnp.float32),
             pltpu.VMEM((tiles, 2 * width + spare, LANES), jnp.float32),
             slots,
             slots,
@@ -404,13 +425,14 @@
             slots,
             pltpu.VMEM((tiles, 2 * width, LANES), jnp.float32),
             pltpu.SemaphoreType.DMA((2, tiles)),
+            pltpu.SemaphoreType.DMA((5,)),
             pltpu.SemaphoreType.DMA((count,)),
             pltpu.SemaphoreType.DMA((count,)),
             pltpu.SemaphoreType.DMA((count,)),
             pltpu.SemaphoreType.DMA((count,)),
         ],
         compiler_params=pltpu.CompilerParams(
-            collective_id=0, has_side_effects=True, vmem_limit_bytes=48 * 1024 * 1024
+            collective_id=0, has_side_effects=True, vmem_limit_bytes=60 * 1024 * 1024
         ),
         name="self_energy",
     )(
@@ -418,7 +440,7 @@
         occupation,
         branch_weight,
         pair_branch,
-        couple_matrix,
+        couple_matrix.transpose(0, 2, 1),
         green_blocks.reshape(2, width, atoms),
     )
     return result.reshape(green_blocks.shape)

time: 47.1 us -> 38.8 us (0.82)
  Pallas kernels: 44.2 us -> 36.8 us
  local copies, waits for them, and re-layouts: 2.65 us -> 1.78 us
    pallas_call x1, Pallas kernels: 44.2 us -> 36.8 us  [on_device(): pl.pallas_call(functools.partial(kernel, n_energy, n_moment, modes), out_...]
    unnamed x12 -> x1, local copies, waits for them, and re-layouts: 2.65 us -> 1.78 us
where the time goes in v1:
time: 38.8 us; the launch traced here: 38.6 us
  Pallas kernels  36.8 us (95%)
  local copies, waits for them, and re-layouts  1.78 us (5%)
    pallas_call x1, Pallas kernels, on_device(): pl.pallas_call(functools.partial(kernel, n_energy, n_moment, modes), out_...  36.8 us
    unnamed x1, local copies, waits for them, and re-layouts  1.78 us

profile of v1, /device:TPU:0, one launch (start us, length us, event | category | flops | bytes accessed | tf_op | source)
XLA Modules:
  0.0 38.6 jit_solution(11448578699324997803)
XLA Ops:
  0.0 36.8 %self_energy.1 = f32[2,200,256]{2,1,0:T(8,128)} custom-call(s32[3]{0:T(128)} %shift_hbm.1, f32[3]{0:T(128)} %occupation_hbm.1, f32[4,3]{1,0:T(4,128)} %weight_hbm.1, s32[4,4]{1,0:T(4,128)} %branch_hbm.1, f32[3,8,100]{2,1,0:T(8,128)} %bitcast.7, f32[2,200,256]{2,1,0:T(8,128)} %bitcast.6), custom_call_target="tpu_custom_call" | custom-call | tf_op jit(solution)/shard_map/self_energy/pallas_call | solution.py:405
  36.8 1.8 %copy.9 = f32[2,1,1,200,256]{4,3,2,1,0:T(8,128)} copy(f32[2,1,1,200,256]{4,3,2,1,0:T(8,128)} %bitcast.5) | data formatting | bytes 819200

commit v2 on v1

v2 whole, which is shorter than its diff:
```python
import functools

import jax
import jax.numpy as jnp
from jax import lax
from jax.experimental import pallas as pl
from jax.experimental.pallas import tpu as pltpu
from jax.sharding import PartitionSpec as P

ORB = 10
PAIRS = ORB * ORB
LANES = 128
ROWS = 8
GROUP = 8
PIECES = LANES // GROUP
QUARTERS = 4
STEPS = PAIRS // QUARTERS
SLOT = 16
THERE = ((0, 15), (15, 10))
HOME = ((0, 10), (10, 15))
UNROLL = 5
MESH = pl.DeviceIdType.MESH


def swap_groups(arrays, lane, width):
    arrays = list(arrays)
    bit = 1
    while bit < len(arrays):
        low = ((lane // width) & bit) == 0
        for p in range(len(arrays)):
            if p & bit:
                continue
            a, b = arrays[p], arrays[p | bit]
            arrays[p] = jnp.where(low, a, pltpu.roll(b, bit * width, 1))
            arrays[p | bit] = jnp.where(low, pltpu.roll(a, LANES - bit * width, 1), b)
        bit *= 2
    return arrays


def total_of(terms):
    while len(terms) > 1:
        paired = [terms[i] + terms[i + 1] for i in range(0, len(terms) - 1, 2)]
        terms = paired + ([terms[-1]] if len(terms) % 2 else [])
    return terms[0]


def piece_rows(piece):
    quarter, kind, part = piece // 4, (piece // 2) % 2, piece % 2
    return kind * 2 * PAIRS + part * PAIRS + quarter


def kernel(
    n_energy,
    n_moment,
    modes,
    shift_hbm,
    occupation_hbm,
    weight_hbm,
    branch_hbm,
    couple_hbm,
    green_ref,
    out_ref,
    shift_ref,
    occupation_ref,
    weight_ref,
    branch_ref,
    couple_ref,
    inside,
    packed_refs,
    arrived_refs,
    mixed,
    coupling,
    coef,
    right_done,
    both_done,
    back_refs,
    returned_refs,
    outside,
    local_sem,
    small_sem,
    send_sem,
    recv_sem,
    own_sem,
    send_back_sem,
    recv_back_sem,
    own_back_sem,
):
    count = n_energy * n_moment
    tiles = green_ref.shape[2] // LANES
    groups = n_moment // QUARTERS
    heights = n_energy // ROWS
    order = sorted(range(n_moment), key=lambda step: -min(step, n_moment - step))
    my_energy = lax.axis_index("energy")
    my_moment = lax.axis_index("momentum")

    def slot_of(energy, moment):
        return pl.multiple_of((moment * n_energy + energy) * SLOT, SLOT)

    def slot_of_rank(rank):
        return slot_of(rank // n_moment, rank % n_moment)

    def for_partners(action):
        def ring(turn, carry):
            energy = lax.rem(my_energy + turn, n_energy)
            for step in order:
                action(energy, lax.rem(my_moment + step, n_moment))
            return carry

        for step in order:
            if step > 0:
                action(my_energy, lax.rem(my_moment + step, n_moment))
        lax.fori_loop(1, n_energy, ring, 0)

    loads = []
    for kind in range(2):
        for tile in range(tiles):
            load = pltpu.make_async_copy(
                green_ref.at[kind, :, pl.ds(tile * LANES, LANES)],
                inside.at[tile, pl.ds(kind * 2 * PAIRS, 2 * PAIRS)],
                local_sem.at[kind, tile],
            )
            load.start()
            loads.append(load)

    small_loads = []
    for index, (source, target) in enumerate(
        (
            (couple_hbm, couple_ref),
            (shift_hbm, shift_ref),
            (occupation_hbm, occupation_ref),
            (weight_hbm, weight_ref),
            (branch_hbm, branch_ref),
        )
    ):
        load = pltpu.make_async_copy(source, target, small_sem.at[index])
        load.start()
        small_loads.append(load)

    barrier = pltpu.get_barrier_semaphore()

    def greet(energy, moment):
        pl.semaphore_signal(
            barrier, inc=1, device_id={"energy": energy, "momentum": moment}, device_id_type=MESH
        )

    for_partners(greet)

    lane = lax.broadcasted_iota(jnp.int32, (ROWS, LANES), 1)

    for load in loads:
        load.wait()

    mine = slot_of(my_energy, my_moment)

    def pack(part):
        begin, rows = THERE[part]

        def pack_tile(tile, carry):
            for place in range(0, rows, ROWS):
                pieces = [
                    inside[
                        tile,
                        pl.ds(piece_rows(p) + QUARTERS * (begin + place), ROWS, stride=QUARTERS),
                        :,
                    ]
                    for p in range(PIECES)
                ]
                for g, value in enumerate(swap_groups(pieces, lane, GROUP)):
                    row = slot_of_rank(tile * PIECES + g) + place
                    packed_refs[part][pl.ds(pl.multiple_of(row, ROWS), ROWS), :] = value
            return carry

        lax.fori_loop(0, tiles, pack_tile, 0)

    def exchange_start(source, target, rows, send, receive, own_sem):
        def start(energy, moment):
            pltpu.make_async_remote_copy(
                src_ref=source.at[pl.ds(slot_of(energy, moment), rows)],
                dst_ref=target.at[pl.ds(mine, rows)],
                send_sem=send,
                recv_sem=receive,
                device_id={"energy": energy, "momentum": moment},
                device_id_type=MESH,
            ).start()

        for_partners(start)
        own = pltpu.make_async_copy(
            source.at[pl.ds(mine, rows)], target.at[pl.ds(mine, rows)], own_sem
        )
        own.start()
        return own

    def wait_all(buffer, rows, semaphore):
        every = buffer.at[pl.ds(0, (count - 1) * rows)]
        pltpu.make_async_copy(every, every, semaphore).wait()

    def start_there(part):
        return exchange_start(
            packed_refs[part],
            arrived_refs[part],
            THERE[part][1],
            send_sem.at[part],
            recv_sem.at[part],
            own_sem.at[part],
        )

    def start_home(part):
        return exchange_start(
            back_refs[part],
            returned_refs[part],
            HOME[part][1],
            send_back_sem.at[part],
            recv_back_sem.at[part],
            own_back_sem.at[part],
        )

    own_there = []
    for part in range(len(THERE)):
        pack(part)
        if part == 0:
            pl.semaphore_wait(barrier, count - 1)
        own_there.append(start_there(part))

    for load in small_loads:
        load.wait()
    spread = (
        lax.broadcasted_iota(jnp.int32, (GROUP, LANES), 1) % GROUP
        == lax.broadcasted_iota(jnp.int32, (GROUP, LANES), 0)
    ).astype(jnp.float32)
    for mode in range(modes):
        wide = lax.dot_general(
            couple_ref[mode],
            spread,
            (((0,), (0,)), ((), ())),
            precision=lax.Precision.HIGHEST,
            preferred_element_type=jnp.float32,
        )
        coupling[pl.ds(mode * PAIRS, PAIRS)] = jnp.broadcast_to(
            wide[:, None, :], (PAIRS, ROWS, LANES)
        )

    lane_moment = lane // (LANES // QUARTERS)
    for mode in range(modes):
        for kg in range(groups):
            for jg in range(groups):
                for turn in range(QUARTERS):
                    value = jnp.zeros((ROWS, LANES), jnp.float32)
                    for kl in range(QUARTERS):
                        k = kg * QUARTERS + kl
                        j = jg * QUARTERS + (kl - turn) % QUARTERS
                        weight = weight_ref[branch_ref[k, j], mode] / n_moment
                        value = jnp.where(lane_moment == kl, weight, value)
                    coef[mode, kg, jg, turn] = value
    kind = ((lane // (2 * GROUP)) % 2).astype(jnp.float32)

    empty = jnp.zeros((n_energy, LANES), jnp.float32)
    for mode in range(modes):
        for kg in range(groups):

            def clear(pair, carry):
                row = pl.multiple_of(pair * 2 * n_energy, ROWS)
                mixed[mode, kg, pl.ds(row, n_energy), :] = empty
                return carry

            lax.fori_loop(0, PAIRS + 1, clear, 0, unroll=True)

    def mix(part):
        begin, rows = THERE[part]
        arrived = arrived_refs[part]

        def mix_step(step, carry):
            for height in range(heights):
                quarters = []
                for jg in range(groups):
                    values = [
                        arrived[
                            pl.ds(
                                ((jg * QUARTERS + jl) * n_energy + height * ROWS) * SLOT + step,
                                ROWS,
                                stride=SLOT,
                            ),
                            :,
                        ]
                        for jl in range(QUARTERS)
                    ]
                    quarters.append(swap_groups(values, lane, LANES // QUARTERS))
                for q in range(QUARTERS):
                    turned = [
                        [quarters[jg][q]]
                        + [
                            pltpu.roll(quarters[jg][q], turn * (LANES // QUARTERS), 1)
                            for turn in range(1, QUARTERS)
                        ]
                        for jg in range(groups)
                    ]
                    pair = QUARTERS * (begin + step) + q
                    row = pl.multiple_of((pair * 2 + 1) * n_energy + height * ROWS, ROWS)
                    for mode in range(modes):
                        for kg in range(groups):
                            mixed[mode, kg, pl.ds(row, ROWS), :] = total_of(
                                [
                                    turned[jg][turn] * coef[mode, kg, jg, turn]
                                    for jg in range(groups)
                                    for turn in range(QUARTERS)
                                ]
                            )
            return carry

        lax.fori_loop(0, rows, mix_step, 0, unroll=UNROLL)

    def multiply_right(part):
        begin, rows = THERE[part]
        for mode in range(modes):
            shift = shift_ref[mode]
            upper_coef = occupation_ref[mode] + 1.0 - kind
            lower_coef = occupation_ref[mode] + kind
            for kg in range(groups):
                for height in range(heights):

                    def right_step(row, carry):
                        values = []
                        for col in range(ORB):
                            first = ((row * ORB + col) * 2 + 1) * n_energy + height * ROWS
                            upper = mixed[mode, kg, pl.ds(first + shift, ROWS), :]
                            lower = mixed[mode, kg, pl.ds(first - shift, ROWS), :]
                            values.append(upper_coef * upper + lower_coef * lower)
                        for n in range(ORB):
                            right_done[mode, kg, height, row * ORB + n] = total_of(
                                [
                                    values[col] * coupling[mode * PAIRS + n * ORB + col]
                                    for col in range(ORB)
                                ]
                            )
                        return carry

                    lax.fori_loop(
                        begin * QUARTERS // ORB,
                        (begin + rows) * QUARTERS // ORB,
                        right_step,
                        0,
                        unroll=2,
                    )

    def multiply_left(part):
        begin, rows = HOME[part]
        back = back_refs[part]
        for kg in range(groups):
            for height in range(heights):

                def left_step(n, carry):
                    values = [
                        [right_done[mode, kg, height, row * ORB + n] for row in range(ORB)]
                        for mode in range(modes)
                    ]
                    for i in range(begin * QUARTERS // ORB, (begin + rows) * QUARTERS // ORB):
                        both_done[kg, height, i * ORB + n] = total_of(
                            [
                                values[mode][row] * coupling[mode * PAIRS + i * ORB + row]
                                for mode in range(modes)
                                for row in range(ORB)
                            ]
                        )
                    return carry

                lax.fori_loop(0, ORB, left_step, 0)

        def unmix_step(step, carry):
            for kg in range(groups):
                for height in range(heights):
                    pair = QUARTERS * (begin + step)
                    values = [both_done[kg, height, pair + q] for q in range(QUARTERS)]
                    for kl, value in enumerate(swap_groups(values, lane, LANES // QUARTERS)):
                        row = ((kg * QUARTERS + kl) * n_energy + height * ROWS) * SLOT + step
                        back[pl.ds(row, ROWS, stride=SLOT), :] = value
            return carry

        lax.fori_loop(0, rows, unmix_step, 0, unroll=UNROLL)

    for part, (_, rows) in enumerate(THERE):
        own_there[part].wait()
        wait_all(arrived_refs[part], rows, recv_sem.at[part])
        mix(part)
        multiply_right(part)
    own_home = []
    for part in range(len(HOME)):
        multiply_left(part)
        own_home.append(start_home(part))
    for part, (_, rows) in enumerate(THERE):
        wait_all(packed_refs[part], rows, send_sem.at[part])

    for part, (begin, rows) in enumerate(HOME):
        own_home[part].wait()
        wait_all(returned_refs[part], rows, recv_back_sem.at[part])

        def unpack(tile, carry):
            for place in range(0, rows, ROWS):
                values = []
                for g in range(PIECES):
                    row = slot_of_rank(tile * PIECES + g) + place
                    values.append(
                        returned_refs[part][pl.ds(pl.multiple_of(row, ROWS), ROWS), :]
                    )
                kept = min(ROWS, rows - place)
                for p, value in enumerate(swap_groups(values, lane, GROUP)):
                    first = piece_rows(p) + QUARTERS * (begin + place)
                    outside[tile, pl.ds(first, kept, stride=QUARTERS), :] = value[:kept]
            return carry

        lax.fori_loop(0, tiles, unpack, 0)

    stores = []
    for kind_index in range(2):
        for tile in range(tiles):
            store = pltpu.make_async_copy(
                outside.at[tile, pl.ds(kind_index * 2 * PAIRS, 2 * PAIRS)],
                out_ref.at[kind_index, :, pl.ds(tile * LANES, LANES)],
                local_sem.at[kind_index, tile],
            )
            store.start()
            stores.append(store)
    for part, (_, rows) in enumerate(HOME):
        wait_all(back_refs[part], rows, send_back_sem.at[part])
    for store in stores:
        store.wait()


def on_device(green_blocks, couple_matrix, occupation, energy_shift, branch_weight, pair_branch):
    n_energy = lax.axis_size("energy")
    n_moment = lax.axis_size("momentum")
    modes = couple_matrix.shape[0]
    width, atoms = green_blocks.shape[3:]
    count = n_energy * n_moment
    tiles = atoms // LANES
    groups = n_moment // QUARTERS
    heights = n_energy // ROWS
    assert green_blocks.shape[1:3] == (1, 1) and width == 2 * PAIRS
    assert couple_matrix.shape[2] == GROUP
    slots = pltpu.VMEM((count * SLOT, LANES), jnp.float32)
    there_slots, home_slots = (slots,) * len(THERE), (slots,) * len(HOME)
    there_sems = pltpu.SemaphoreType.DMA((len(THERE),))
    home_sems = pltpu.SemaphoreType.DMA((len(HOME),))
    spare = QUARTERS * ROWS
    result = pl.pallas_call(
        functools.partial(kernel, n_energy, n_moment, modes),
        out_shape=jax.ShapeDtypeStruct((2, width, atoms), jnp.float32),
        in_specs=[pl.BlockSpec(memory_space=pl.ANY)] * 6,
        out_specs=pl.BlockSpec(memory_space=pl.ANY),
        scratch_shapes=[
            pltpu.SMEM(energy_shift.shape, jnp.int32),
            pltpu.SMEM(occupation.shape, jnp.float32),
            pltpu.SMEM(branch_weight.shape, jnp.float32),
            pltpu.SMEM(pair_branch.shape, jnp.int32),
            pltpu.VMEM((modes, GROUP, PAIRS), jnp.float32),
            pltpu.VMEM((tiles, 2 * width + spare, LANES), jnp.float32),
            there_slots,
            there_slots,
            pltpu.VMEM((modes, groups, (2 * PAIRS + 1) * n_energy, LANES), jnp.float32),
            pltpu.VMEM((modes * PAIRS, ROWS, LANES), jnp.float32),
            pltpu.VMEM((modes, groups, groups, QUARTERS, ROWS, LANES), jnp.float32),
            pltpu.VMEM((modes, groups, heights, PAIRS, ROWS, LANES), jnp.float32),
            pltpu.VMEM((groups, heights, PAIRS, ROWS, LANES), jnp.float32),
            home_slots,
            home_slots,
            pltpu.VMEM((tiles, 2 * width, LANES), jnp.float32),
            pltpu.SemaphoreType.DMA((2, tiles)),
            pltpu.SemaphoreType.DMA((5,)),
            there_sems,
            there_sems,
            there_sems,
            home_sems,
            home_sems,
            home_sems,
        ],
        compiler_params=pltpu.CompilerParams(
            collective_id=0, has_side_effects=True, vmem_limit_bytes=60 * 1024 * 1024
        ),
        name="self_energy",
    )(
        energy_shift,
        occupation,
        branch_weight,
        pair_branch,
        couple_matrix.transpose(0, 2, 1),
        green_blocks.reshape(2, width, atoms),
    )
    return result.reshape(green_blocks.shape)


def solution(mesh):
    in_specs = (
        P(None, "energy", "momentum", None, None),
        P(None, None, ("energy", "momentum")),
        P(),
        P(),
        P(),
        P(),
    )
    out_specs = P(None, "energy", "momentum", None, None)
    return jax.shard_map(
        on_device, mesh=mesh, in_specs=in_specs, out_specs=out_specs, check_vma=False
    )
```

time: 38.8 us -> 34.8 us (0.90)
  Pallas kernels: 36.8 us -> 32.8 us
    pallas_call x1, Pallas kernels: 36.8 us -> 32.8 us  [on_device(): pl.pallas_call(functools.partial(kernel, n_energy, n_moment, modes), out_...]
where the time goes in v2:
time: 34.8 us; the launch traced here: 34.6 us
  Pallas kernels  32.8 us (94%)
  local copies, waits for them, and re-layouts  1.78 us (5%)
    pallas_call x1, Pallas kernels, on_device(): pl.pallas_call(functools.partial(kernel, n_energy, n_moment, modes), out_...  32.8 us
    unnamed x1, local copies, waits for them, and re-layouts  1.78 us

profile of v2, /device:TPU:0, one launch (start us, length us, event | category | flops | bytes accessed | tf_op | source)
XLA Modules:
  0.0 34.6 jit_solution(10660345614830873078)
XLA Ops:
  0.0 32.8 %self_energy.1 = f32[2,200,256]{2,1,0:T(8,128)} custom-call(s32[3]{0:T(128)} %shift_hbm.1, f32[3]{0:T(128)} %occupation_hbm.1, f32[4,3]{1,0:T(4,128)} %weight_hbm.1, s32[4,4]{1,0:T(4,128)} %branch_hbm.1, f32[3,8,100]{2,1,0:T(8,128)} %bitcast.7, f32[2,200,256]{2,1,0:T(8,128)} %bitcast.6), custom_call_target="tpu_custom_call" | custom-call | tf_op jit(solution)/shard_map/self_energy/pallas_call | solution.py:443
  32.8 1.8 %copy.9 = f32[2,1,1,200,256]{4,3,2,1,0:T(8,128)} copy(f32[2,1,1,200,256]{4,3,2,1,0:T(8,128)} %bitcast.5) | data formatting | bytes 819200

commit v3 on v2

--- a/solution.py
+++ b/solution.py
@@ -16,8 +16,8 @@
 QUARTERS = 4
 STEPS = PAIRS // QUARTERS
 SLOT = 16
-THERE = ((0, 15), (15, 10))
-HOME = ((0, 10), (10, 15))
+THERE = ((0, 10), (10, 10), (20, 5))
+HOME = ((0, 5), (5, 10), (15, 10))
 UNROLL = 5
 MESH = pl.DeviceIdType.MESH
 
@@ -362,7 +362,7 @@
                         )
                     return carry
 
-                lax.fori_loop(0, ORB, left_step, 0)
+                lax.fori_loop(0, ORB, left_step, 0, unroll=2)
 
         def unmix_step(step, carry):
             for kg in range(groups):
@@ -442,7 +442,7 @@
     spare = QUARTERS * ROWS
     result = pl.pallas_call(
         functools.partial(kernel, n_energy, n_moment, modes),
-        out_shape=jax.ShapeDtypeStruct((2, width, atoms), jnp.float32),
+        out_shape=pltpu.VMEM((2, width, atoms), jnp.float32),
         in_specs=[pl.BlockSpec(memory_space=pl.ANY)] * 6,
         out_specs=pl.BlockSpec(memory_space=pl.ANY),
         scratch_shapes=[

time: 34.8 us -> 32.7 us (0.940)
  local copies, waits for them, and re-layouts: 1.78 us -> 0.75 us
  Pallas kernels: 32.8 us -> 31.8 us
    unnamed x1, local copies, waits for them, and re-layouts: 1.78 us -> 0.75 us
    pallas_call x1, Pallas kernels: 32.8 us -> 31.8 us  [on_device(): pl.pallas_call(functools.partial(kernel, n_energy, n_moment, modes), out_...]
where the time goes in v3:
time: 32.7 us; the launch traced here: 32.6 us
  Pallas kernels  31.8 us (97%)
  local copies, waits for them, and re-layouts  0.75 us (2%)
    pallas_call x1, Pallas kernels, on_device(): pl.pallas_call(functools.partial(kernel, n_energy, n_moment, modes), out_...  31.8 us
    unnamed x1, local copies, waits for them, and re-layouts  0.75 us

profile of v3, /device:TPU:0, one launch (start us, length us, event | category | flops | bytes accessed | tf_op | source)
XLA Modules:
  0.0 32.6 jit_solution(5019087810813372425)
XLA Ops:
  0.0 31.8 %self_energy.1 = f32[2,200,256]{2,1,0:T(8,128)S(1)} custom-call(s32[3]{0:T(128)} %shift_hbm.1, f32[3]{0:T(128)} %occupation_hbm.1, f32[4,3]{1,0:T(4,128)} %weight_hbm.1, s32[4,4]{1,0:T(4,128)} %branch_hbm.1, f32[3,8,100]{2,1,0:T(8,128)} %bitcast.7, f32[2,200,256]{2,1,0:T(8,128)} %bitcast.6), custom_call_target="tpu_custom_call" | custom-call | tf_op jit(solution)/shard_map/self_energy/pallas_call | solution.py:443
  31.9 0.8 %copy.9 = f32[2,1,1,200,256]{4,3,2,1,0:T(8,128)} copy(f32[2,1,1,200,256]{4,3,2,1,0:T(8,128)S(1)} %bitcast.5) | data formatting | bytes 819200

commit v4 on v3

--- a/solution.py
+++ b/solution.py
@@ -17,7 +17,7 @@
 STEPS = PAIRS // QUARTERS
 SLOT = 16
 THERE = ((0, 10), (10, 10), (20, 5))
-HOME = ((0, 5), (5, 10), (15, 10))
+HOME = ((0, 5), (5, 15), (20, 5))
 UNROLL = 5
 MESH = pl.DeviceIdType.MESH
 
@@ -89,7 +89,6 @@
     tiles = green_ref.shape[2] // LANES
     groups = n_moment // QUARTERS
     heights = n_energy // ROWS
-    order = sorted(range(n_moment), key=lambda step: -min(step, n_moment - step))
     my_energy = lax.axis_index("energy")
     my_moment = lax.axis_index("momentum")
 
@@ -99,17 +98,23 @@
     def slot_of_rank(rank):
         return slot_of(rank // n_moment, rank % n_moment)
 
+    def across(flip):
+        moment, bit = my_moment, 1
+        while bit <= flip:
+            if flip & bit:
+                moment = moment + bit - 2 * bit * ((my_moment // bit) % 2)
+            bit *= 2
+        return moment
+
     def for_partners(action):
-        def ring(turn, carry):
-            energy = lax.rem(my_energy + turn, n_energy)
-            for step in order:
-                action(energy, lax.rem(my_moment + step, n_moment))
-            return carry
-
-        for step in order:
-            if step > 0:
-                action(my_energy, lax.rem(my_moment + step, n_moment))
-        lax.fori_loop(1, n_energy, ring, 0)
+        for flip in reversed(range(n_moment)):
+            moment = across(flip)
+
+            def ring(turn, carry):
+                action(lax.rem(my_energy + turn, n_energy), moment)
+                return carry
+
+            lax.fori_loop(0 if flip else 1, n_energy, ring, 0, unroll=2)
 
     loads = []
     for kind in range(2):
@@ -388,6 +393,13 @@
     for part, (_, rows) in enumerate(THERE):
         wait_all(packed_refs[part], rows, send_sem.at[part])
 
+    def store_of(index, tile):
+        return pltpu.make_async_copy(
+            outside.at[tile, pl.ds(index * 2 * PAIRS, 2 * PAIRS)],
+            out_ref.at[index, :, pl.ds(pl.multiple_of(tile * LANES, LANES), LANES)],
+            local_sem.at[index, tile],
+        )
+
     for part, (begin, rows) in enumerate(HOME):
         own_home[part].wait()
         wait_all(returned_refs[part], rows, recv_back_sem.at[part])
@@ -404,24 +416,22 @@
                 for p, value in enumerate(swap_groups(values, lane, GROUP)):
                     first = piece_rows(p) + QUARTERS * (begin + place)
                     outside[tile, pl.ds(first, kept, stride=QUARTERS), :] = value[:kept]
+            if part == len(HOME) - 1:
+                for index in range(2):
+                    store_of(index, tile).start()
             return carry
 
         lax.fori_loop(0, tiles, unpack, 0)
 
-    stores = []
-    for kind_index in range(2):
-        for tile in range(tiles):
-            store = pltpu.make_async_copy(
-                outside.at[tile, pl.ds(kind_index * 2 * PAIRS, 2 * PAIRS)],
-                out_ref.at[kind_index, :, pl.ds(tile * LANES, LANES)],
-                local_sem.at[kind_index, tile],
-            )
-            store.start()
-            stores.append(store)
     for part, (_, rows) in enumerate(HOME):
         wait_all(back_refs[part], rows, send_back_sem.at[part])
-    for store in stores:
-        store.wait()
+
+    def finish(tile, carry):
+        for index in range(2):
+            store_of(index, tile).wait()
+        return carry
+
+    lax.fori_loop(0, tiles, finish, 0)
 
 
 def on_device(green_blocks, couple_matrix, occupation, energy_shift, branch_weight, pair_branch):

time: 32.7 us -> 33.4 us (1.021)
  Pallas kernels: 31.8 us -> 32.5 us
    pallas_call x1, Pallas kernels: 31.8 us -> 32.5 us  [on_device(): pl.pallas_call(functools.partial(kernel, n_energy, n_moment, modes), out_...]
where the time goes in v4:
time: 33.4 us; the launch traced here: 33.3 us
  Pallas kernels  32.5 us (97%)
  local copies, waits for them, and re-layouts  0.75 us (2%)
    pallas_call x1, Pallas kernels, on_device(): pl.pallas_call(functools.partial(kernel, n_energy, n_moment, modes), out_...  32.5 us
    unnamed x1, local copies, waits for them, and re-layouts  0.75 us

profile of v4, /device:TPU:0, one launch (start us, length us, event | category | flops | bytes accessed | tf_op | source)
XLA Modules:
  0.0 33.3 jit_solution(9062441070504481372)
XLA Ops:
  0.0 32.5 %self_energy.1 = f32[2,200,256]{2,1,0:T(8,128)S(1)} custom-call(s32[3]{0:T(128)} %shift_hbm.1, f32[3]{0:T(128)} %occupation_hbm.1, f32[4,3]{1,0:T(4,128)} %weight_hbm.1, s32[4,4]{1,0:T(4,128)} %branch_hbm.1, f32[3,8,100]{2,1,0:T(8,128)} %bitcast.7, f32[2,200,256]{2,1,0:T(8,128)} %bitcast.6), custom_call_target="tpu_custom_call" | custom-call | tf_op jit(solution)/shard_map/self_energy/pallas_call | solution.py:453
  32.5 0.8 %copy.9 = f32[2,1,1,200,256]{4,3,2,1,0:T(8,128)} copy(f32[2,1,1,200,256]{4,3,2,1,0:T(8,128)S(1)} %bitcast.5) | data formatting | bytes 819200

commit v5 on v4

--- a/solution.py
+++ b/solution.py
@@ -98,23 +98,20 @@
     def slot_of_rank(rank):
         return slot_of(rank // n_moment, rank % n_moment)
 
-    def across(flip):
-        moment, bit = my_moment, 1
-        while bit <= flip:
-            if flip & bit:
-                moment = moment + bit - 2 * bit * ((my_moment // bit) % 2)
-            bit *= 2
-        return moment
+    order = sorted(range(n_moment), key=lambda step: -min(step, n_moment - step))
+    stride = n_energy // n_moment
 
     def for_partners(action):
-        for flip in reversed(range(n_moment)):
-            moment = across(flip)
-
-            def ring(turn, carry):
-                action(lax.rem(my_energy + turn, n_energy), moment)
-                return carry
-
-            lax.fori_loop(0 if flip else 1, n_energy, ring, 0, unroll=2)
+        def ring(turn, carry, steps=tuple(order)):
+            for step in steps:
+                action(
+                    lax.rem(my_energy + turn + stride * step, n_energy),
+                    lax.rem(my_moment + step, n_moment),
+                )
+            return carry
+
+        ring(0, 0, [step for step in order if step > 0])
+        lax.fori_loop(1, n_energy, ring, 0)
 
     loads = []
     for kind in range(2):

time: 33.4 us -> 33.4 us (level)
  no operation moved by 1% of the time
where the time goes in v5:
time: 33.4 us; the launch traced here: 33.3 us
  Pallas kernels  32.5 us (97%)
  local copies, waits for them, and re-layouts  0.75 us (2%)
    pallas_call x1, Pallas kernels, on_device(): pl.pallas_call(functools.partial(kernel, n_energy, n_moment, modes), out_...  32.5 us
    unnamed x1, local copies, waits for them, and re-layouts  0.75 us

profile of v5, /device:TPU:0, one launch (start us, length us, event | category | flops | bytes accessed | tf_op | source)
XLA Modules:
  0.0 33.3 jit_solution(5949496754798312727)
XLA Ops:
  0.0 32.5 %self_energy.1 = f32[2,200,256]{2,1,0:T(8,128)S(1)} custom-call(s32[3]{0:T(128)} %shift_hbm.1, f32[3]{0:T(128)} %occupation_hbm.1, f32[4,3]{1,0:T(4,128)} %weight_hbm.1, s32[4,4]{1,0:T(4,128)} %branch_hbm.1, f32[3,8,100]{2,1,0:T(8,128)} %bitcast.7, f32[2,200,256]{2,1,0:T(8,128)} %bitcast.6), custom_call_target="tpu_custom_call" | custom-call | tf_op jit(solution)/shard_map/self_energy/pallas_call | solution.py:450
  32.5 0.8 %copy.9 = f32[2,1,1,200,256]{4,3,2,1,0:T(8,128)} copy(f32[2,1,1,200,256]{4,3,2,1,0:T(8,128)S(1)} %bitcast.5) | data formatting | bytes 819200

commit v6 on v5

--- a/solution.py
+++ b/solution.py
@@ -17,7 +17,7 @@
 STEPS = PAIRS // QUARTERS
 SLOT = 16
 THERE = ((0, 10), (10, 10), (20, 5))
-HOME = ((0, 5), (5, 15), (20, 5))
+HOME = ((0, 5), (5, 10), (15, 10))
 UNROLL = 5
 MESH = pl.DeviceIdType.MESH
 
@@ -99,13 +99,12 @@
         return slot_of(rank // n_moment, rank % n_moment)
 
     order = sorted(range(n_moment), key=lambda step: -min(step, n_moment - step))
-    stride = n_energy // n_moment
 
     def for_partners(action):
         def ring(turn, carry, steps=tuple(order)):
             for step in steps:
                 action(
-                    lax.rem(my_energy + turn + stride * step, n_energy),
+                    lax.rem(my_energy + turn, n_energy),
                     lax.rem(my_moment + step, n_moment),
                 )
             return carry
@@ -343,28 +342,39 @@
                         unroll=2,
                     )
 
+    def sum_left(first, last, rows, add):
+        for kg in range(groups):
+            for height in range(heights):
+
+                def left_step(n, carry):
+                    values = [
+                        [right_done[mode, kg, height, row * ORB + n] for row in rows]
+                        for mode in range(modes)
+                    ]
+                    for i in range(first, last):
+                        terms = [
+                            values[mode][index] * coupling[mode * PAIRS + i * ORB + row]
+                            for mode in range(modes)
+                            for index, row in enumerate(rows)
+                        ]
+                        if add:
+                            terms.append(both_done[kg, height, i * ORB + n])
+                        both_done[kg, height, i * ORB + n] = total_of(terms)
+                    return carry
+
+                lax.fori_loop(0, ORB, left_step, 0, unroll=2)
+
+    last_row = THERE[-1][0] * QUARTERS // ORB
+
     def multiply_left(part):
         begin, rows = HOME[part]
         back = back_refs[part]
-        for kg in range(groups):
-            for height in range(heights):
-
-                def left_step(n, carry):
-                    values = [
-                        [right_done[mode, kg, height, row * ORB + n] for row in range(ORB)]
-                        for mode in range(modes)
-                    ]
-                    for i in range(begin * QUARTERS // ORB, (begin + rows) * QUARTERS // ORB):
-                        both_done[kg, height, i * ORB + n] = total_of(
-                            [
-                                values[mode][row] * coupling[mode * PAIRS + i * ORB + row]
-                                for mode in range(modes)
-                                for row in range(ORB)
-                            ]
-                        )
-                    return carry
-
-                lax.fori_loop(0, ORB, left_step, 0, unroll=2)
+        sum_left(
+            begin * QUARTERS // ORB,
+            (begin + rows) * QUARTERS // ORB,
+            range(last_row, ORB),
+            True,
+        )
 
         def unmix_step(step, carry):
             for kg in range(groups):
@@ -379,6 +389,8 @@
         lax.fori_loop(0, rows, unmix_step, 0, unroll=UNROLL)
 
     for part, (_, rows) in enumerate(THERE):
+        if part == len(THERE) - 1:
+            sum_left(0, ORB, range(last_row), False)
         own_there[part].wait()
         wait_all(arrived_refs[part], rows, recv_sem.at[part])
         mix(part)

time: 33.4 us -> 33.4 us (level)
  no operation moved by 1% of the time
where the time goes in v6:
time: 33.4 us; the launch traced here: 33.2 us
  Pallas kernels  32.5 us (97%)
  local copies, waits for them, and re-layouts  0.75 us (2%)
    pallas_call x1, Pallas kernels, on_device(): pl.pallas_call(functools.partial(kernel, n_energy, n_moment, modes), out_...  32.5 us
    unnamed x1, local copies, waits for them, and re-layouts  0.75 us

profile of v6, /device:TPU:0, one launch (start us, length us, event | category | flops | bytes accessed | tf_op | source)
XLA Modules:
  0.0 33.2 jit_solution(12805424205962363452)
XLA Ops:
  0.0 32.5 %self_energy.1 = f32[2,200,256]{2,1,0:T(8,128)S(1)} custom-call(s32[3]{0:T(128)} %shift_hbm.1, f32[3]{0:T(128)} %occupation_hbm.1, f32[4,3]{1,0:T(4,128)} %weight_hbm.1, s32[4,4]{1,0:T(4,128)} %branch_hbm.1, f32[3,8,100]{2,1,0:T(8,128)} %bitcast.7, f32[2,200,256]{2,1,0:T(8,128)} %bitcast.6), custom_call_target="tpu_custom_call" | custom-call | tf_op jit(solution)/shard_map/self_energy/pallas_call | solution.py:462
  32.5 0.8 %copy.9 = f32[2,1,1,200,256]{4,3,2,1,0:T(8,128)} copy(f32[2,1,1,200,256]{4,3,2,1,0:T(8,128)S(1)} %bitcast.5) | data formatting | bytes 819200
